TPU v7x, 128 devices: a whole 4x4x4 slice. The times are simulated.
128 devices in a mesh: row: 4 (over x_hi, core), reader: 32 (over x_lo, z, y).
Axes of the slice: x: 4 (x_hi: 2, x_lo: 2; x = x_hi * 2 + x_lo), y: 4, z: 4, core: 2. Of those that a mesh axis runs over, the one named last changes fastest.
Arguments:
- records: bfloat16 [4, 32, 256, 4096], P('row', None, 'reader'), may hold values from -6 to 6
- lengths: int32 [4, 32], replicated, may hold values from 1 to 256, as said below
- assignment: int32 [4, 32], replicated, may hold values from 0 to 31, as said below
- segment_ids: int32 [4, 32, 256], replicated, may hold values from 0 to 11, never falling along the last dimension, each value on 1 to 64 neighbouring positions
- norm_gain: float32 [4096], replicated, may hold values from 0.6 to 6
- w_qkv: bfloat16 [4096, 4, 1280], P('reader', 'row'), may hold values from -0.09375 to 0.09375
- w_out: bfloat16 [4096, 4, 1024], P('reader', 'row'), may hold values from -0.09375 to 0.09375
- score_weights: float32 [4096], replicated, may hold values from -0.09375 to 0.09375
Outputs:
- hidden_out: bfloat16 [28672, 4096], P('reader', 'row')
- record_scores: float32 [32, 4], P('reader')
Inputs may be any that keep to these rules, and one draw needn't show every extreme that they name: `assignment`: each row names every scorer shard exactly once. For every scorer shard the lengths of the records that name it, one from each row, sum to 896; some record has 256. `segment_ids`: along a record the document numbers never fall.
All inputs are finite; a program needn't handle non-finite values.
Results may differ from a plain program's by a relative error of at most 0.015.
The roundings to bfloat16 on the way count: a program that leaves them out, or rounds other values in their place, can miss the bound.
Values may be sent and summed in bfloat16 or wider, within the bound.
No kernel may reach another device: no remote copies, remote signals or barrier semaphores. Data moves between devices by JAX's collectives and lax.ppermute only.
A program may use at most 128 MiB of HBM per device.

v0:
```python
import math
import jax
import jax.numpy as jnp
from jax import lax
from jax.sharding import PartitionSpec as P

HS = 128
GROUP = 8
RECLEN = 256
ROPE_BASE = 500000.0


def rotary(values, cosine, sine):
    half = values.shape[-1] // 2
    shape = (values.shape[0],) + (1,) * (values.ndim - 2) + (half,)
    cosine = cosine.reshape(shape)
    sine = sine.reshape(shape)
    first = values[..., :half]
    second = values[..., half:]
    return jnp.concatenate(
        [first * cosine - second * sine, second * cosine + first * sine], axis=-1
    )


def masked_softmax(logits, allowed):
    held = jnp.where(allowed, logits, -1e30)
    top = jnp.max(held, axis=-1, keepdims=True)
    weights = jnp.where(allowed, jnp.exp(held - top), 0.0)
    return weights / jnp.sum(weights, axis=-1, keepdims=True)


def on_device(records, lengths, assignment, segment_ids, norm_gain, w_qkv, w_out, score_weights):
    row_count = lax.axis_size("row")
    reader_count = lax.axis_size("reader")
    row_index = lax.axis_index("row")
    reader_index = lax.axis_index("reader")
    slot_count = records.shape[2]
    width = records.shape[3]
    local_heads = w_qkv.shape[1]
    tok_rows = row_count * RECLEN - RECLEN // 2
    row_ids = jnp.arange(row_count, dtype=jnp.int32)
    chosen = jnp.argmax(assignment == reader_index, axis=1)
    record_lens = jnp.take_along_axis(lengths, chosen[:, None], axis=1)[:, 0]
    ends = jnp.cumsum(record_lens)
    starts = ends - record_lens
    place = jnp.arange(tok_rows, dtype=jnp.int32)
    owner = jnp.sum((place[:, None] >= ends[None, :-1]).astype(jnp.int32), axis=1)
    matches = owner[:, None] == row_ids[None, :]
    within = place - jnp.sum(jnp.where(matches, starts[None, :], 0), axis=1)
    picked = jnp.sum(jnp.where(matches, chosen[None, :], 0), axis=1)
    segs = segment_ids[owner, picked, within]
    own_assign = lax.dynamic_index_in_dim(assignment, row_index, 0, keepdims=False)
    readers = jnp.arange(reader_count, dtype=jnp.int32)
    outgoing = jnp.argmax(own_assign[None, :] == readers[:, None], axis=1)
    send_block = records[0][outgoing]
    arrived = lax.all_to_all(send_block, "reader", split_axis=0, concat_axis=0, tiled=True)
    own_record = arrived.reshape(1, reader_count * slot_count, width)
    gathered = lax.all_gather(own_record, "row", axis=0, tiled=True)
    packed = gathered.reshape(row_count * RECLEN, width)[owner * RECLEN + within]
    packed_f = packed.astype(jnp.float32)
    scale = lax.rsqrt(jnp.mean(packed_f * packed_f, axis=1, keepdims=True) + 1e-05)
    normed = (packed_f * scale * norm_gain).astype(jnp.bfloat16)
    full_qkv, full_out = (
        lax.all_gather(w_qkv, "reader", axis=0, tiled=True),
        lax.all_gather(w_out, "reader", axis=0, tiled=True),
    )
    projected = jnp.dot(normed, full_qkv.reshape(width, -1), preferred_element_type=jnp.float32)
    projected = projected.reshape(tok_rows, local_heads, GROUP + 2, HS)
    inv_freq = ROPE_BASE ** (-(jnp.arange(HS // 2, dtype=jnp.float32) * 2.0 / HS))
    angle = within.astype(jnp.float32)[:, None] * inv_freq[None, :]
    cosine = jnp.cos(angle)
    sine = jnp.sin(angle)
    queries = rotary(projected[:, :, :GROUP], cosine, sine).astype(jnp.bfloat16)
    keys = rotary(projected[:, :, GROUP], cosine, sine).astype(jnp.bfloat16)
    values = projected[:, :, GROUP + 1].astype(jnp.bfloat16)
    allowed = (
        (owner[:, None] == owner[None, :])
        & (segs[:, None] == segs[None, :])
        & (place[None, :] <= place[:, None])
    )
    logits = jnp.einsum("qhgd,khd->hgqk", queries, keys, preferred_element_type=jnp.float32) * (
        1.0 / math.sqrt(HS)
    )
    probs = masked_softmax(logits, allowed[None, None]).astype(jnp.bfloat16)
    mixed = jnp.einsum("hgqk,khd->qhgd", probs, values, preferred_element_type=jnp.float32).astype(
        jnp.bfloat16
    )
    mixed_flat = mixed.reshape(tok_rows, local_heads * GROUP * HS)
    partial_value = jnp.einsum(
        "tj,dj->td", mixed_flat, full_out.reshape(width, -1), preferred_element_type=jnp.float32
    )
    summed = lax.psum_scatter(
        partial_value.astype(jnp.bfloat16), "row", scatter_dimension=1, tiled=True
    ).astype(jnp.float32)
    col_width = width // row_count
    packed_cols = lax.dynamic_slice_in_dim(packed_f, row_index * col_width, col_width, 1)
    total = packed_cols + summed
    hidden_out = total.astype(jnp.bfloat16)
    score_cols = lax.dynamic_slice_in_dim(score_weights, row_index * col_width, col_width, 0)
    token_scores = jnp.dot(total, score_cols, precision=lax.Precision.HIGHEST)
    record_part = jnp.dot(
        token_scores, matches.astype(jnp.float32), precision=lax.Precision.HIGHEST
    )
    record_total = lax.psum(record_part, "row")
    record_scores = (record_total / record_lens.astype(jnp.float32))[None, :]
    return (hidden_out, record_scores)


def solution(mesh):
    in_specs = (
        P("row", None, "reader", None),
        P(),
        P(),
        P(),
        P(),
        P("reader", "row", None),
        P("reader", "row", None),
        P(),
    )
    out_specs = (P("reader", "row"), P("reader", None))
    return jax.shard_map(
        on_device, mesh=mesh, in_specs=in_specs, out_specs=out_specs, check_vma=False
    )
```

profile of v0, /device:TPU:1, one launch (start us, length us, event | category | flops | bytes accessed | tf_op | source)
XLA Modules:
  0.0 561.5 jit_solution(11207179706539714900)
XLA Ops:
  7.3 0.8 dynamic-slice_bitcast_fusion
  8.1 0.6 iota_reduce_fusion
  8.8 2.0 gather_fusion
  10.8 36.0 %all_to_all.5 = bf16[32,8,4096]{2,1,0:T(8,128)(2,1)} all-to-all(bf16[32,8,4096]{2,1,0:T(8,128)(2,1)} %gather_fusion), channel_id=1, replica_groups=mesh['row'=4,'reader'=32] {'reader'}, dimensions={0} | all-to-all | bytes 4194304 | tf_op jit(solution)/shard_map/all_to_all | solution.py:56
  46.9 0.7 all-gather.6.cloned.1.call-update
  47.6 0.7 all-gather.8.cloned.1.call-update
  48.4 0.6 iota_reduce_fusion.1
  49.1 0.6 gather_fusion.3
  49.7 0.2 reduce-window.4
  50.2 9.0 %gather_fusion.2 = s32[896]{0:T(1024)S(1)} fusion(s32[4,32,256]{2,1,0:T(8,128)S(1)} %copy-done.3, s32[896]{0:T(1024)S(1)} %get-tuple-element.6), kind=kCustom, calls=%fused_computation.2 | custom fusion | bytes 17920 | tf_op jit(solution)/shard_map/gather | solution.py:51
  59.2 0.9 multiply_cosine_fusion
  60.1 1.2 fusion.15
  61.3 48.4 %all-gather.4.cloned.1.call-done = bf16[4,256,4096]{2,1,0:T(8,128)(2,1)} async-done(((bf16[1,256,4096]{2,1,0:T(8,128)(2,1)}), bf16[4,256,4096]{2,1,0:T(8,128)(2,1)}) %all-gather.4.cloned.1.call-update) | async-done | bytes 8388624 | tf_op jit(solution)/shard_map/all_gather | solution.py:58
  109.7 19.4 %gather_fusion.1 = bf16[896,4096]{1,0:T(8,128)(2,1)} fusion(bf16[1024,4096]{1,0:T(8,128)(2,1)} %bitcast.91, s32[1024]{0:T(1024)S(1)} %pad_clamp_fusion), kind=kCustom, calls=%fused_computation.1 | custom fusion | bytes 14683648 | tf_op jit(solution)/shard_map/gather | solution.py:59
  129.2 4.6 multiply_reduce_fusion
  133.8 130.7 %all-gather.6.cloned.1.call-done = bf16[4096,1,1280]{2,0,1:T(8,128)(2,1)} async-done(((bf16[128,1,1280]{2,0,1:T(8,128)(2,1)}), bf16[4096,1,1280]{2,0,1:T(8,128)(2,1)}) %all-gather.6.cloned.1.call-update) | async-done | bytes 10485776 | tf_op jit(solution)/shard_map/all_gather | solution.py:64
  264.6 14.3 %copy.22 = bf16[1280,4096]{1,0:T(8,128)(2,1)} copy(bf16[1280,4096]{0,1:T(8,128)(2,1)} %bitcast.92) | data formatting | bytes 20971520 | tf_op jit(solution)/shard_map/dot_general | solution.py:67
  278.9 15.1 %fusion.18 = f32[896,1,10,128]{0,3,2,1:T(8,128)S(1)} fusion(bf16[10,128,4096]{2,1,0:T(8,128)(2,1)} %bitcast.93, f32[4096]{0:T(1024)S(1)} %copy-done.5, f32[896]{0:T(1024)S(1)} %add_rsqrt_fusion, bf16[896,4096]{1,0:T(8,128)(2,1)} %gather_fusion.1), kind=kOutput, calls=%fused_computation.26 | convolution fusion | flops 9409921024 | bytes 22433280 | tf_op jit(solution)/shard_map/dot_general | solution.py:67
  294.0 0.9 fusion.44
  294.9 0.5 fusion.29
  295.5 11.1 %fusion = (f32[8,896]{1,0:T(8,128)S(1)}, f32[896,896,8]{1,0,2:T(8,128)}) fusion(pred[896,896]{0,1:T(8,128)(4,1)S(1)} %fusion.15, bf16[896,8,64]{0,2,1:T(8,128)(2,1)S(1)} %get-tuple-element.11, bf16[896,8,64]{0,2,1:T(8,128)(2,1)S(1)} %get-tuple-element.10, bf16[896,64]{0,1:T(8,128)(2,1)S(1)} %get-tuple-element.13, bf16[896,64]{0,1:T(8,128)(2,1)S(1)} %get-tuple-element.12), kind=kOutput, calls=%fused_computation.7 | convolution fusion | flops 1667556352 | bytes 28585984 | tf_op jit(solution)/shard_map/qhgd,khd->hgqk/dot_general | solution.py:81
  306.6 12.1 %fusion.1 = f32[8,896]{1,0:T(8,128)S(1)} fusion(f32[896,896,8]{1,0,2:T(8,128)} %get-tuple-element.17, f32[8,896]{1,0:T(8,128)S(1)} %get-tuple-element.16, pred[896,896]{0,1:T(8,128)(4,1)S(1)} %fusion.15), kind=kLoop, calls=%fused_computation.8 | loop fusion | flops 32105472 | bytes 26550272 | tf_op jit(solution)/shard_map/reduce_sum | solution.py:29
  318.6 14.9 %fusion.25 = bf16[128,8,896]{2,0,1:T(8,128)(2,1)} fusion(f32[8,896]{1,0:T(8,128)S(1)} %fusion.1, f32[8,896]{1,0:T(8,128)S(1)} %get-tuple-element.16, f32[896,896,8]{1,0,2:T(8,128)} %get-tuple-element.17, pred[896,896]{0,1:T(8,128)(4,1)S(1)} %fusion.15, f32[896,1,10,128]{0,3,2,1:T(8,128)S(1)} %fusion.18), kind=kOutput, calls=%fused_computation.33 | convolution fusion | flops 1683619840 | bytes 28614656 | tf_op jit(solution)/shard_map/hgqk,khd->qhgd/dot_general | solution.py:85
  333.5 97.7 %all-gather.8.cloned.1.call-done = bf16[4096,1,1024]{2,0,1:T(8,128)(2,1)} async-done(((bf16[128,1,1024]{2,0,1:T(8,128)(2,1)}), bf16[4096,1,1024]{2,0,1:T(8,128)(2,1)}) %all-gather.8.cloned.1.call-update) | async-done | bytes 8388624 | tf_op jit(solution)/shard_map/all_gather | solution.py:65
  431.2 12.6 %fusion.12 = bf16[896,4096]{1,0:T(8,128)(2,1)} fusion(bf16[896,1024]{0,1:T(8,128)(2,1)} %bitcast.96, bf16[4096,1,1024]{2,0,1:T(8,128)(2,1)} %all-gather.8.cloned.1.call-done), kind=kOutput, calls=%fused_computation.20 | convolution fusion | flops 7519862784 | bytes 17563648 | tf_op jit(solution)/shard_map/tj,dj->td/dot_general | solution.py:89
  443.9 10.4 %convert_element_type.57 = f32[896,4096]{1,0:T(8,128)} convert(bf16[896,4096]{1,0:T(8,128)(2,1)} %gather_fusion.1) | non-fusion elementwise | flops 3670016 | bytes 22020096 | tf_op jit(solution)/shard_map/convert_element_type | solution.py:60
  454.3 82.3 %reduce-scatter.2.cloned.1.call-done = bf16[896,1024]{1,0:T(8,128)(2,1)} async-done(((bf16[896,4096]{1,0:T(8,128)(2,1)}), bf16[896,1024]{1,0:T(8,128)(2,1)}) %reduce-scatter.2.cloned.1.call-update) | async-done | bytes 1835024 | tf_op jit(solution)/shard_map/reduce_scatter | solution.py:92
  536.7 5.9 %fusion.28 = f32[896,1]{0,1:T(1,128)S(1)} fusion(f32[1024,1]{0,1:T(1,128)S(1)} %bitcast.95, bf16[896,1024]{1,0:T(8,128)(2,1)} %reduce-scatter.2.cloned.1.call-done, f32[896,4096]{1,0:T(8,128)} %convert_element_type.57, s32[]{:T(128)} %select_n.96), kind=kOutput, calls=%fused_computation.34 | convolution fusion | flops 12845056 | bytes 5513216 | tf_op jit(solution)/shard_map/dot_general | solution.py:100
  542.6 0.1 convolution_bitcast_fusion
  542.7 7.2 %psum.7 = f32[4]{0:T(128)S(1)} all-reduce(f32[4]{0:T(128)S(1)} %convolution_bitcast_fusion), channel_id=1, replica_groups=mesh['row'=4,'reader'=32] {'row'}, use_global_device_ids=true, to_apply=%region_10.11 | all-reduce | flops 4 | bytes 32 | tf_op jit(solution)/shard_map/psum | solution.py:104
  549.9 0.5 fusion.57
  550.4 4.5 fusion.17
  (37 shorter events, 0.6 us)
Async XLA Ops:
  7.2 1.6 copy-start
  7.2 41.2 %copy-start.4 = (s32[4,32]{1,0:T(4,128)S(1)}, s32[4,32]{1,0:T(4,128)}, u32[]{:S(2)}) copy-start(s32[4,32]{1,0:T(4,128)} %param.10) | copy-start | bytes 1540
  7.2 41.9 %copy-start.2 = (s32[4,32]{1,0:T(4,128)S(1)}, s32[4,32]{1,0:T(4,128)}, u32[]{:S(2)}) copy-start(s32[4,32]{1,0:T(4,128)} %param.9) | copy-start | bytes 1540
  7.2 43.0 %copy-start.3 = (s32[4,32,256]{2,1,0:T(8,128)S(1)}, s32[4,32,256]{2,1,0:T(8,128)}, u32[]{:S(2)}) copy-start(s32[4,32,256]{2,1,0:T(8,128)} %param.11) | copy-start | bytes 393220
  7.2 102.5 %all-gather.4.cloned.1.call-start = ((), (), s32[]{:S(2)}) async-start(), calls=%async_computation.2 | async-start | bytes 10485760 | tf_op jit(solution)/shard_map/all_gather | solution.py:58
  46.8 217.7 %all-gather.6.cloned.1.call-start = ((), (), s32[]{:S(2)}) async-start(), calls=%async_computation.3 | async-start | bytes 10813440 | tf_op jit(solution)/shard_map/all_gather | solution.py:64
  47.6 383.6 %all-gather.8.cloned.1.call-start = ((), (), s32[]{:S(2)}) async-start(), calls=%async_computation.4 | async-start | bytes 8650752 | tf_op jit(solution)/shard_map/all_gather | solution.py:65
  48.3 488.3 %reduce-scatter.2.cloned.1.call-start = ((), (), s32[]{:S(2)}) async-start(), calls=%async_computation.5 | async-start | bytes 9175040 | tf_op jit(solution)/shard_map/reduce_scatter | solution.py:92
  264.6 14.3 %copy-start.5 = (f32[4096]{0:T(1024)S(1)}, f32[4096]{0:T(1024)}, u32[]{:S(2)}) copy-start(f32[4096]{0:T(1024)} %param.12) | copy-start | bytes 49156
  443.9 92.8 %dynamic-slice-start = ((f32[4096]{0:T(1024)}, s32[]{:T(128)}), f32[1024]{0:T(1024)S(1)}, s32[]{:S(2)}) async-start(f32[4096]{0:T(1024)} %param.15, s32[]{:T(128)} %select_n.96), calls=%async_computation.6 | async-start | bytes 8704 | tf_op jit(solution)/shard_map/dynamic_slice | solution.py:99
  443.9 111.0 %copy-start.1 = (bf16[1,32,8,4096]{3,2,1,0:T(8,128)(2,1)S(1)}, bf16[1,32,8,4096]{3,2,1,0:T(8,128)(2,1)}, u32[]{:S(2)}) copy-start(bf16[1,32,8,4096]{3,2,1,0:T(8,128)(2,1)} %param.8) | copy-start | bytes 6291460
Sparse Core Ops, SparseCore 0:
  47.0 62.7 all-gather.3
  111.4 153.1 all-gather.5
  266.2 164.9 all-gather.7
  444.0 92.6 reduce-scatter.1
where the time goes:
time: 562 us; the launch traced here: 561 us
  waiting for transfers between devices  361 us (64%)
  matrix products  59.7 us (11%)
  local copies, waits for them, and re-layouts  46.4 us (8%)
  blocking collectives  43.2 us (8%)
  other arithmetic  37.4 us (7%)
  between operations  14 us (2%)
    all_gather x1, waiting for transfers between devices, on_device(): lax.all_gather(w_qkv, 'reader', axis=0, tiled=True)  131 us
    all_gather x1, waiting for transfers between devices, on_device(): lax.all_gather(w_out, 'reader', axis=0, tiled=True)  97.7 us
    reduce_scatter x1, waiting for transfers between devices, on_device(): lax.psum_scatter(partial_value.astype(jnp.bfloat16), 'row', scatter_dimen...  82.3 us
    all_gather x1, waiting for transfers between devices, on_device(): gathered = lax.all_gather(own_record, 'row', axis=0, tiled=True)  48.4 us
    all_to_all x1, blocking collectives, on_device(): lax.all_to_all(send_block, 'reader', split_axis=0, concat_axis=0, tiled=T...  36 us
    gather x1, local copies, waits for them, and re-layouts, on_device(): gathered.reshape(row_count * RECLEN, width)[owner * RECLEN + within]  19.4 us
    dot_general x1, matrix products, on_device(): jnp.dot(normed, full_qkv.reshape(width, -1), preferred_element_type=jnp.f...  15.1 us
    dot_general x1, matrix products, on_device(): jnp.einsum('hgqk,khd->qhgd', probs, values, preferred_element_type=jnp.fl...  14.9 us
  transfers between devices with their start and end apart: 4, of which 4 were waited for; matrix products, arithmetic and copies ran while one was open for 21% of the time, Pallas kernels for 0%

commit v1 on v0

--- a/solution.py
+++ b/solution.py
@@ -55,7 +55,9 @@
     send_block = records[0][outgoing]
     arrived = lax.all_to_all(send_block, "reader", split_axis=0, concat_axis=0, tiled=True)
     own_record = arrived.reshape(1, reader_count * slot_count, width)
-    gathered = lax.all_gather(own_record, "row", axis=0, tiled=True)
+    gathered = jnp.concatenate(
+        lax.all_to_all(jnp.stack([own_record] * lax.axis_size("row")), "row", 0, 0), axis=0
+    )
     packed = gathered.reshape(row_count * RECLEN, width)[owner * RECLEN + within]
     packed_f = packed.astype(jnp.float32)
     scale = lax.rsqrt(jnp.mean(packed_f * packed_f, axis=1, keepdims=True) + 1e-05)

time: 562 us -> 529 us (0.941)
  waiting for transfers between devices: 361 us -> 304 us
  blocking collectives: 43.2 us -> 55.6 us
  starting transfers between devices: 0.16 us -> 6.98 us
    all_to_all x0 -> x1, waiting for transfers between devices: none -> 167 us  [on_device(): lax.all_to_all(jnp.stack([own_record] * lax.axis_size('row')), 'row', 0, 0)]
    all_gather x1, waiting for transfers between devices: 131 us -> 0.02 us  [on_device(): lax.all_gather(w_qkv, 'reader', axis=0, tiled=True)]
    all_gather x1 -> x0, waiting for transfers between devices: 48.4 us -> none  [on_device(): gathered = lax.all_gather(own_record, 'row', axis=0, tiled=True)]
    all_gather x1, waiting for transfers between devices: 97.7 us -> 53.3 us  [on_device(): lax.all_gather(w_out, 'reader', axis=0, tiled=True)]
    all_to_all x1, blocking collectives: 36 us -> 48.4 us  [on_device(): lax.all_to_all(send_block, 'reader', split_axis=0, concat_axis=0, tiled=T...]
    all_to_all x0 -> x1, starting transfers between devices: none -> 6.9 us  [on_device(): lax.all_to_all(jnp.stack([own_record] * lax.axis_size('row')), 'row', 0, 0)]
  transfers between devices with their start and end apart: 4 -> 4, of which waited for: 4 -> 3; matrix products, arithmetic and copies ran while one was open for 21% -> 23% of each run, Pallas kernels for 0% -> 0%
where the time goes in v1:
time: 529 us; the launch traced here: 528 us
  waiting for transfers between devices  304 us (57%)
  matrix products  59.8 us (11%)
  blocking collectives  55.6 us (11%)
  local copies, waits for them, and re-layouts  50.5 us (10%)
  other arithmetic  37.4 us (7%)
  between operations  13.9 us (3%)
  starting transfers between devices  6.98 us (1%)
    all_to_all x1, waiting for transfers between devices, on_device(): lax.all_to_all(jnp.stack([own_record] * lax.axis_size('row')), 'row', 0, 0)  167 us
    reduce_scatter x1, waiting for transfers between devices, on_device(): lax.psum_scatter(partial_value.astype(jnp.bfloat16), 'row', scatter_dimen...  82.2 us
    all_gather x1, waiting for transfers between devices, on_device(): lax.all_gather(w_out, 'reader', axis=0, tiled=True)  53.3 us
    all_to_all x1, blocking collectives, on_device(): lax.all_to_all(send_block, 'reader', split_axis=0, concat_axis=0, tiled=T...  48.4 us
    gather x1, local copies, waits for them, and re-layouts, on_device(): gathered.reshape(row_count * RECLEN, width)[owner * RECLEN + within]  19.4 us
    dot_general x1, matrix products, on_device(): jnp.dot(normed, full_qkv.reshape(width, -1), preferred_element_type=jnp.f...  15.2 us
    dot_general x1, matrix products, on_device(): jnp.einsum('hgqk,khd->qhgd', probs, values, preferred_element_type=jnp.fl...  14.9 us
    dot_general x1, local copies, waits for them, and re-layouts, on_device(): jnp.dot(normed, full_qkv.reshape(width, -1), preferred_element_type=jnp.f...  14.3 us
  transfers between devices with their start and end apart: 4, of which 3 were waited for; matrix products, arithmetic and copies ran while one was open for 23% of the time, Pallas kernels for 0%

profile of v1, /device:TPU:1, one launch (start us, length us, event | category | flops | bytes accessed | tf_op | source)
XLA Modules:
  0.0 528.1 jit_solution(9527262755189528749)
XLA Ops:
  7.2 0.7 all-gather.3.cloned.1.call-update
  7.9 0.7 dynamic-slice_bitcast_fusion
  8.6 0.6 iota_reduce_fusion
  9.3 2.0 gather_fusion
  11.2 48.4 %all_to_all.10 = bf16[32,8,4096]{2,1,0:T(8,128)(2,1)S(1)} all-to-all(bf16[32,8,4096]{2,1,0:T(8,128)(2,1)} %gather_fusion), channel_id=1, replica_groups=mesh['row'=4,'reader'=32] {'reader'}, dimensions={0} | all-to-all | bytes 4194304 | tf_op jit(solution)/shard_map/all_to_all | solution.py:56
  59.7 4.3 stack.3
  64.0 6.9 %all-to-all-start.1 = ((bf16[4,1,256,4096]{3,2,1,0:T(8,128)(2,1)}), bf16[4,1,256,4096]{3,2,1,0:T(8,128)(2,1)}, u32[]{:S(2)}, u32[]{:S(2)}) async-start(bf16[4,1,256,4096]{3,2,1,0:T(8,128)(2,1)} %stack.3), calls=%async_computation.1 | async-start | bytes 16777216 | tf_op jit(solution)/shard_map/all_to_all | solution.py:59
  70.9 0.7 all-gather.5.cloned.1.call-update
  71.7 0.6 iota_reduce_fusion.1
  72.4 0.6 gather_fusion.3
  73.0 0.2 reduce-window.4
  73.5 9.0 %gather_fusion.2 = s32[896]{0:T(1024)S(1)} fusion(s32[4,32,256]{2,1,0:T(8,128)S(1)} %copy-done.3, s32[896]{0:T(1024)S(1)} %get-tuple-element.6), kind=kCustom, calls=%fused_computation.2 | custom fusion | bytes 17920 | tf_op jit(solution)/shard_map/gather | solution.py:51
  82.5 0.9 multiply_cosine_fusion
  83.4 1.2 fusion.15
  84.6 166.9 %all-to-all-done.1 = bf16[4,1,256,4096]{3,2,1,0:T(8,128)(2,1)} async-done(((bf16[4,1,256,4096]{3,2,1,0:T(8,128)(2,1)}), bf16[4,1,256,4096]{3,2,1,0:T(8,128)(2,1)}, u32[]{:S(2)}, u32[]{:S(2)}) %all-to-all-start.1) | async-done | bytes 8388640 | tf_op jit(solution)/shard_map/all_to_all | solution.py:59
  251.6 19.4 %gather_fusion.1 = bf16[896,4096]{1,0:T(8,128)(2,1)} fusion(bf16[1024,4096]{1,0:T(8,128)(2,1)} %bitcast.3, s32[1024]{0:T(1024)S(1)} %pad_clamp_fusion), kind=kCustom, calls=%fused_computation.1 | custom fusion | bytes 14683648 | tf_op jit(solution)/shard_map/gather | solution.py:61
  271.0 4.6 multiply_reduce_fusion
  275.7 14.3 %copy.22 = bf16[1280,4096]{1,0:T(8,128)(2,1)} copy(bf16[1280,4096]{0,1:T(8,128)(2,1)} %bitcast.91) | data formatting | bytes 20971520 | tf_op jit(solution)/shard_map/dot_general | solution.py:69
  290.0 15.2 %fusion.18 = f32[896,1,10,128]{0,3,2,1:T(8,128)S(1)} fusion(bf16[10,128,4096]{2,1,0:T(8,128)(2,1)} %bitcast.92, f32[4096]{0:T(1024)S(1)} %copy-done.5, f32[896]{0:T(1024)S(1)} %add_rsqrt_fusion, bf16[896,4096]{1,0:T(8,128)(2,1)} %gather_fusion.1), kind=kOutput, calls=%fused_computation.26 | convolution fusion | flops 9409921024 | bytes 22433280 | tf_op jit(solution)/shard_map/dot_general | solution.py:69
  305.2 0.9 fusion.44
  306.1 0.5 fusion.29
  306.7 11.1 %fusion = (f32[8,896]{1,0:T(8,128)S(1)}, f32[896,896,8]{1,0,2:T(8,128)}) fusion(pred[896,896]{0,1:T(8,128)(4,1)S(1)} %fusion.15, bf16[896,8,64]{0,2,1:T(8,128)(2,1)S(1)} %get-tuple-element.11, bf16[896,8,64]{0,2,1:T(8,128)(2,1)S(1)} %get-tuple-element.10, bf16[896,64]{0,1:T(8,128)(2,1)S(1)} %get-tuple-element.13, bf16[896,64]{0,1:T(8,128)(2,1)S(1)} %get-tuple-element.12), kind=kOutput, calls=%fused_computation.7 | convolution fusion | flops 1667556352 | bytes 28585984 | tf_op jit(solution)/shard_map/qhgd,khd->hgqk/dot_general | solution.py:83
  317.8 12.1 %fusion.1 = f32[8,896]{1,0:T(8,128)S(1)} fusion(f32[896,896,8]{1,0,2:T(8,128)} %get-tuple-element.17, f32[8,896]{1,0:T(8,128)S(1)} %get-tuple-element.16, pred[896,896]{0,1:T(8,128)(4,1)S(1)} %fusion.15), kind=kLoop, calls=%fused_computation.8 | loop fusion | flops 32105472 | bytes 26550272 | tf_op jit(solution)/shard_map/reduce_sum | solution.py:29
  329.9 14.9 %fusion.25 = bf16[128,8,896]{2,0,1:T(8,128)(2,1)} fusion(f32[8,896]{1,0:T(8,128)S(1)} %fusion.1, f32[8,896]{1,0:T(8,128)S(1)} %get-tuple-element.16, f32[896,896,8]{1,0,2:T(8,128)} %get-tuple-element.17, pred[896,896]{0,1:T(8,128)(4,1)S(1)} %fusion.15, f32[896,1,10,128]{0,3,2,1:T(8,128)S(1)} %fusion.18), kind=kOutput, calls=%fused_computation.33 | convolution fusion | flops 1683619840 | bytes 28614656 | tf_op jit(solution)/shard_map/hgqk,khd->qhgd/dot_general | solution.py:87
  344.7 53.3 %all-gather.5.cloned.1.call-done = bf16[4096,1,1024]{2,0,1:T(8,128)(2,1)} async-done(((bf16[128,1,1024]{2,0,1:T(8,128)(2,1)}), bf16[4096,1,1024]{2,0,1:T(8,128)(2,1)}) %all-gather.5.cloned.1.call-update) | async-done | bytes 8388624 | tf_op jit(solution)/shard_map/all_gather | solution.py:67
  398.0 12.6 %fusion.12 = bf16[896,4096]{1,0:T(8,128)(2,1)} fusion(bf16[896,1024]{0,1:T(8,128)(2,1)} %bitcast.95, bf16[4096,1,1024]{2,0,1:T(8,128)(2,1)} %all-gather.5.cloned.1.call-done), kind=kOutput, calls=%fused_computation.20 | convolution fusion | flops 7519862784 | bytes 17563648 | tf_op jit(solution)/shard_map/tj,dj->td/dot_general | solution.py:91
  410.7 10.4 %convert_element_type.57 = f32[896,4096]{1,0:T(8,128)} convert(bf16[896,4096]{1,0:T(8,128)(2,1)} %gather_fusion.1) | non-fusion elementwise | flops 3670016 | bytes 22020096 | tf_op jit(solution)/shard_map/convert_element_type | solution.py:62
  421.1 82.2 %reduce-scatter.2.cloned.1.call-done = bf16[896,1024]{1,0:T(8,128)(2,1)} async-done(((bf16[896,4096]{1,0:T(8,128)(2,1)}), bf16[896,1024]{1,0:T(8,128)(2,1)}) %reduce-scatter.2.cloned.1.call-update) | async-done | bytes 1835024 | tf_op jit(solution)/shard_map/reduce_scatter | solution.py:94
  503.3 5.9 %fusion.28 = f32[896,1]{0,1:T(1,128)S(1)} fusion(f32[1024,1]{0,1:T(1,128)S(1)} %bitcast.94, bf16[896,1024]{1,0:T(8,128)(2,1)} %reduce-scatter.2.cloned.1.call-done, f32[896,4096]{1,0:T(8,128)} %convert_element_type.57, s32[]{:T(128)} %select_n.96), kind=kOutput, calls=%fused_computation.34 | convolution fusion | flops 12845056 | bytes 5513216 | tf_op jit(solution)/shard_map/dot_general | solution.py:102
  509.3 7.2 %psum.7 = f32[4]{0:T(128)S(1)} all-reduce(f32[4]{0:T(128)S(1)} %convolution_bitcast_fusion), channel_id=1, replica_groups=mesh['row'=4,'reader'=32] {'row'}, use_global_device_ids=true, to_apply=%region_10.11 | all-reduce | flops 4 | bytes 32 | tf_op jit(solution)/shard_map/psum | solution.py:106
  516.5 0.5 fusion.57
  517.1 4.5 fusion.17
  (37 shorter events, 0.6 us)
Async XLA Ops:
  7.2 2.1 copy-start
  7.2 268.5 %all-gather.3.cloned.1.call-start = ((), (), s32[]{:S(2)}) async-start(), calls=%async_computation.3 | async-start | bytes 10813440 | tf_op jit(solution)/shard_map/all_gather | solution.py:66
  64.0 7.7 %copy-start.4 = (s32[4,32]{1,0:T(4,128)S(1)}, s32[4,32]{1,0:T(4,128)}, u32[]{:S(2)}) copy-start(s32[4,32]{1,0:T(4,128)} %param.10) | copy-start | bytes 1540
  64.0 8.4 %copy-start.2 = (s32[4,32]{1,0:T(4,128)S(1)}, s32[4,32]{1,0:T(4,128)}, u32[]{:S(2)}) copy-start(s32[4,32]{1,0:T(4,128)} %param.9) | copy-start | bytes 1540
  64.0 9.5 %copy-start.3 = (s32[4,32,256]{2,1,0:T(8,128)S(1)}, s32[4,32,256]{2,1,0:T(8,128)}, u32[]{:S(2)}) copy-start(s32[4,32,256]{2,1,0:T(8,128)} %param.11) | copy-start | bytes 393220
  64.0 187.6 %all-to-all-start.1 = ((bf16[4,1,256,4096]{3,2,1,0:T(8,128)(2,1)}), bf16[4,1,256,4096]{3,2,1,0:T(8,128)(2,1)}, u32[]{:S(2)}, u32[]{:S(2)}) async-start(bf16[4,1,256,4096]{3,2,1,0:T(8,128)(2,1)} %stack.3), calls=%async_computation.1 | async-start | bytes 16777216 | tf_op jit(solution)/shard_map/all_to_all | solution.py:59
  70.9 327.1 %all-gather.5.cloned.1.call-start = ((), (), s32[]{:S(2)}) async-start(), calls=%async_computation.4 | async-start | bytes 8650752 | tf_op jit(solution)/shard_map/all_gather | solution.py:67
  71.6 431.7 %reduce-scatter.2.cloned.1.call-start = ((), (), s32[]{:S(2)}) async-start(), calls=%async_computation.5 | async-start | bytes 9175040 | tf_op jit(solution)/shard_map/reduce_scatter | solution.py:94
  275.7 14.3 %copy-start.5 = (f32[4096]{0:T(1024)S(1)}, f32[4096]{0:T(1024)}, u32[]{:S(2)}) copy-start(f32[4096]{0:T(1024)} %param.12) | copy-start | bytes 49156
  410.7 92.6 %dynamic-slice-start = ((f32[4096]{0:T(1024)}, s32[]{:T(128)}), f32[1024]{0:T(1024)S(1)}, s32[]{:S(2)}) async-start(f32[4096]{0:T(1024)} %param.15, s32[]{:T(128)} %select_n.96), calls=%async_computation.6 | async-start | bytes 8704 | tf_op jit(solution)/shard_map/dynamic_slice | solution.py:101
  410.7 110.9 %copy-start.1 = (bf16[1,32,8,4096]{3,2,1,0:T(8,128)(2,1)S(1)}, bf16[1,32,8,4096]{3,2,1,0:T(8,128)(2,1)}, u32[]{:S(2)}) copy-start(bf16[1,32,8,4096]{3,2,1,0:T(8,128)(2,1)} %param.8) | copy-start | bytes 6291460
Sparse Core Ops, SparseCore 0:
  9.7 238.1 all-gather.2
  249.5 148.4 all-gather.4
  410.8 92.4 reduce-scatter.1
